TPU v7x, 32 devices: a whole 2x2x4 slice. The times are simulated.
32 devices in a mesh: img: 4 (over y, x), ch: 8 (over z, core).
Axes of the slice: x: 2, y: 2, z: 4, core: 2. Of those that a mesh axis runs over, the one named last changes fastest.
Arguments:
- images_in: bfloat16 [256, 49, 2048], P('img'), may hold values from -6 to 6
- labels: int32 [256], P(('img', 'ch')), may hold values from 0 to 999
- loss_wt: int32 [256], P(('img', 'ch')), may hold values from 1 to 32
- placement: int32 [4, 64], P('img'), may hold values from 0 to 63, each once within a row
- w_one: float32 [2048, 512], P(None, 'ch'), may hold values from -0.125 to 0.125
- mom_one: float32 [2048, 512], P(None, 'ch'), may hold values from -0.0029296875 to 0.0029296875
- avg_one: float32 [2048, 512], P(None, 'ch'), may hold values from -0.125 to 0.125
- mask_one: int32 [2048, 512], P(None, 'ch'), may hold values 0 or 1
- rank_one: int32 [2048, 512], P(None, 'ch'), may hold values from 0 to 99
- first_norm_params: float32 [2, 512], P(None, 'ch'), may hold values from 0.5 to 1.5
- mom_bn_one: float32 [2, 512], P(None, 'ch'), may hold values from -0.001953125 to 0.001953125
- avg_bn_one: float32 [2, 512], P(None, 'ch'), may hold values from 0.5 to 1.5
- w_two: float32 [2359296], P(('img', 'ch')), may hold values from -0.09375 to 0.09375
- mom_two: float32 [2359296], P(('img', 'ch')), may hold values from -0.01171875 to 0.01171875
- avg_two: float32 [2359296], P(('img', 'ch')), may hold values from -0.09375 to 0.09375
- mask_two: int32 [2359296], P(('img', 'ch')), may hold values 0 or 1
- rank_two: int32 [2359296], P(('img', 'ch')), may hold values from 0 to 99
- second_norm_params: float32 [2, 512], replicated, may hold values from 0.5 to 1.5
- mom_bn_two: float32 [2, 512], replicated, may hold values from -0.01953125 to 0.01953125
- avg_bn_two: float32 [2, 512], replicated, may hold values from 0.5 to 1.5
- w_head: float32 [512000], P(('img', 'ch')), may hold values from -0.75 to 0.75
- mom_head: float32 [512000], P(('img', 'ch')), may hold values from -0.0029296875 to 0.0029296875
- avg_head: float32 [512000], P(('img', 'ch')), may hold values from -0.75 to 0.75
Outputs:
- loss: float32 [], replicated
- new_w_one: float32 [2048, 512], P(None, 'ch')
- new_mom_one: float32 [2048, 512], P(None, 'ch')
- new_avg_one: float32 [2048, 512], P(None, 'ch')
- new_mask_one: int32 [2048, 512], P(None, 'ch')
- copy_w_one: bfloat16 [2048, 512], P(None, 'ch')
- new_bn_one: float32 [2, 512], P(None, 'ch')
- new_mom_bn_one: float32 [2, 512], P(None, 'ch')
- new_avg_bn_one: float32 [2, 512], P(None, 'ch')
- new_w_two: float32 [2359296], P(('img', 'ch'))
- new_mom_two: float32 [2359296], P(('img', 'ch'))
- new_avg_two: float32 [2359296], P(('img', 'ch'))
- new_mask_two: int32 [2359296], P(('img', 'ch'))
- copy_w_two: bfloat16 [2359296], P(('img', 'ch'))
- new_bn_two: float32 [2, 512], replicated
- new_mom_bn_two: float32 [2, 512], replicated
- new_avg_bn_two: float32 [2, 512], replicated
- new_w_head: float32 [512000], P(('img', 'ch'))
- new_mom_head: float32 [512000], P(('img', 'ch'))
- new_avg_head: float32 [512000], P(('img', 'ch'))
- copy_w_head: bfloat16 [512000], P(('img', 'ch'))
Inputs may be any that keep to these rules, and one draw needn't show every extreme that they name: `placement`: each row is a permutation of 0 to 63.
All inputs are finite; a program needn't handle non-finite values. No bound on the sum of `mask_one` or of `mask_two` on one device may be relied on, other than what follows from the above.
Results may differ from a plain program's by a relative error of at most 0.013.
Values may be sent and summed in bfloat16 or wider, within the bound.
A program may use at most 512 MiB of HBM per device.

v0:
```python
import math
import jax
import jax.numpy as jnp
from jax import lax
from jax.sharding import PartitionSpec as P

SIDE = 7
PIX = 49
DROP = 10
GROW = 10
EPS = 1e-05
MOMENTUM = 0.5


def advance(weight, grad, velocity, rate):
    velocity = MOMENTUM * velocity + grad
    return (weight - rate * (grad + MOMENTUM * velocity), velocity)


def dense_update(weight, grad, velocity, average, rate):
    moved, velocity = advance(weight, grad, velocity, rate)
    return (moved, velocity, 0.5 * average + 0.5 * moved)


def sparse_update(weight, grad, velocity, average, mask, rank, rate):
    moved, velocity = advance(weight, grad, velocity, rate)
    kept = (mask == 1) & (rank >= DROP)
    grown = (mask == 0) & (rank < GROW)
    new_mask = jnp.where(kept | grown, 1, 0).astype(jnp.int32)
    weight = jnp.where(kept, moved, 0.0)
    velocity = jnp.where(kept, velocity, 0.0)
    average = 0.5 * average + 0.5 * weight
    return (weight, velocity, average, new_mask, weight.astype(jnp.bfloat16))


def silu_slope(value):
    sigma = jax.nn.sigmoid(value)
    return sigma * (1.0 + value * (1.0 - sigma))


def apply_batch_norm(z, sums, squares, element_count):
    mean = sums / element_count
    inverse_deviation = lax.rsqrt(squares / element_count - mean * mean + EPS)
    return ((z - mean) * inverse_deviation, inverse_deviation)


def batch_norm_backward(
    norm_gain,
    inverse_deviation,
    output_gradient,
    standardized_input,
    bias_gradient_sum,
    gain_gradient_sum,
    element_count,
):
    return (
        norm_gain
        * inverse_deviation
        * (
            output_gradient
            - bias_gradient_sum / element_count
            - standardized_input * gain_gradient_sum / element_count
        )
    )


def contract_rows(left, right):
    return jnp.einsum("pk,pc->kc", left, right, preferred_element_type=jnp.float32)


def shards(
    images_in,
    labels,
    loss_wt,
    placement,
    w_one,
    mom_one,
    avg_one,
    mask_one,
    rank_one,
    first_norm_params,
    mom_bn_one,
    avg_bn_one,
    w_two,
    mom_two,
    avg_two,
    mask_two,
    rank_two,
    second_norm_params,
    mom_bn_two,
    avg_bn_two,
    w_head,
    mom_head,
    avg_head,
):
    n_img = lax.axis_size("img")
    n_ch = lax.axis_size("ch")
    group = images_in.shape[0]
    element_count = labels.shape[0]
    width = second_norm_params.shape[1]
    classes = w_head.shape[0] * n_img * n_ch // width
    images = element_count * n_img * n_ch
    slot_info = jnp.stack([labels.astype(jnp.float32), loss_wt.astype(jnp.float32)])
    slot_info = lax.all_gather(slot_info, "ch", axis=1, tiled=True)
    own = lax.axis_index("ch") * element_count + jnp.arange(element_count, dtype=jnp.int32)
    fills = placement[0][None, :] == own[:, None]
    labels_f, weights = jnp.sum(jnp.where(fills[None], slot_info[:, None, :], 0.0), axis=2)
    labels = labels_f.astype(jnp.int32)
    kernel_part = (w_two * mask_two.astype(jnp.float32)).astype(jnp.bfloat16)
    kernel = lax.all_gather(kernel_part, ("img", "ch"), axis=0, tiled=True)
    head = lax.all_gather(w_head.astype(jnp.bfloat16), ("img", "ch"), axis=0, tiled=True)
    kernel = kernel.reshape(9 * width, width)
    head = head.reshape(width, classes)
    rows = images_in.transpose(1, 0, 2).reshape(PIX * group, images_in.shape[2])
    filt_one = (w_one * mask_one.astype(jnp.float32)).astype(jnp.bfloat16)
    first_conv_output = jnp.dot(rows, filt_one, preferred_element_type=jnp.float32)
    first_feature_sum, first_squares_sum, total = lax.psum(
        (
            jnp.sum(first_conv_output, axis=0),
            jnp.sum(first_conv_output * first_conv_output, axis=0),
            jnp.sum(slot_info[1]),
        ),
        "img",
    )
    first_element_count = group * PIX * n_img
    first_standardized_input, first_inverse_deviation = apply_batch_norm(
        first_conv_output, first_feature_sum, first_squares_sum, first_element_count
    )
    first_norm_output = first_norm_params[0] * first_standardized_input + first_norm_params[1]
    act = jax.nn.silu(first_norm_output).astype(jnp.bfloat16).reshape(PIX, group, -1)
    act_in = lax.all_to_all(act, "ch", split_axis=1, concat_axis=2, tiled=True)
    padded = jnp.pad(
        act_in.reshape(SIDE, SIDE, element_count, width), ((1, 1), (1, 1), (0, 0), (0, 0))
    )
    patches = jnp.concatenate(
        [
            padded[tap // 3 : tap // 3 + SIDE, tap % 3 : tap % 3 + SIDE].reshape(
                PIX * element_count, width
            )
            for tap in range(9)
        ],
        axis=1,
    )
    second_conv_output = jnp.dot(patches, kernel, preferred_element_type=jnp.float32)
    second_feature_sum, second_squares_sum = lax.psum(
        (
            jnp.sum(second_conv_output, axis=0),
            jnp.sum(second_conv_output * second_conv_output, axis=0),
        ),
        ("img", "ch"),
    )
    second_element_count = images * PIX
    second_standardized_input, second_inverse_deviation = apply_batch_norm(
        second_conv_output, second_feature_sum, second_squares_sum, second_element_count
    )
    second_norm_output = second_norm_params[0] * second_standardized_input + second_norm_params[1]
    pooled = jnp.mean(jax.nn.silu(second_norm_output).reshape(PIX, element_count, width), axis=0)
    pooled_low = pooled.astype(jnp.bfloat16)
    logits = jnp.dot(pooled_low, head, preferred_element_type=jnp.float32)
    top = jnp.max(logits, axis=1, keepdims=True)
    expd = jnp.exp(logits - top)
    denom = jnp.sum(expd, axis=1, keepdims=True)
    lse = top[:, 0] + jnp.log(denom[:, 0])
    onehot = labels[:, None] == jnp.arange(classes, dtype=jnp.int32)[None, :]
    picked = jnp.sum(jnp.where(onehot, logits, 0.0), axis=1)
    share = weights / total
    partial_loss_value = jnp.sum(share * (lse - picked))
    d_logits = (share[:, None] * (expd / denom - onehot.astype(jnp.float32))).astype(jnp.bfloat16)
    g_head = contract_rows(pooled_low, d_logits)
    d_pooled = jnp.einsum("ic,kc->ik", d_logits, head, preferred_element_type=jnp.float32)
    d_act = jnp.broadcast_to(d_pooled[None] / PIX, (PIX, element_count, width)).reshape(
        PIX * element_count, width
    )
    second_output_gradient = d_act * silu_slope(second_norm_output)
    second_shift_bias, second_norm_gain, loss = lax.psum(
        (
            jnp.sum(second_output_gradient, axis=0),
            jnp.sum(second_output_gradient * second_standardized_input, axis=0),
            partial_loss_value,
        ),
        ("img", "ch"),
    )
    second_preact_gradient = batch_norm_backward(
        second_norm_params[0],
        second_inverse_deviation,
        second_output_gradient,
        second_standardized_input,
        second_shift_bias,
        second_norm_gain,
        second_element_count,
    ).astype(jnp.bfloat16)
    d_patches = jnp.einsum(
        "pc,kc->pk", second_preact_gradient, kernel, preferred_element_type=jnp.float32
    )
    d_pad = 0.0
    for tap in range(9):
        piece = d_patches[:, tap * width : (tap + 1) * width].reshape(
            SIDE, SIDE, element_count, width
        )
        up, left = (tap // 3, tap % 3)
        d_pad = d_pad + jnp.pad(piece, ((up, 2 - up), (left, 2 - left), (0, 0), (0, 0)))
    d_act_in = d_pad[1:-1, 1:-1].astype(jnp.bfloat16).reshape(PIX, element_count, width)
    d_act_one = lax.all_to_all(d_act_in, "ch", split_axis=2, concat_axis=1, tiled=True)
    g_kernel = contract_rows(patches, second_preact_gradient)
    d_act_one = d_act_one.reshape(PIX * group, -1).astype(jnp.float32)
    first_output_gradient = d_act_one * silu_slope(first_norm_output)
    first_shift_bias, first_norm_gain = lax.psum(
        (
            jnp.sum(first_output_gradient, axis=0),
            jnp.sum(first_output_gradient * first_standardized_input, axis=0),
        ),
        "img",
    )
    first_preact_gradient = batch_norm_backward(
        first_norm_params[0],
        first_inverse_deviation,
        first_output_gradient,
        first_standardized_input,
        first_shift_bias,
        first_norm_gain,
        first_element_count,
    ).astype(jnp.bfloat16)
    g_filt = lax.psum(
        contract_rows(rows, first_preact_gradient).astype(jnp.bfloat16), "img"
    ).astype(jnp.float32)
    g_one = g_filt * mask_one.astype(jnp.float32)
    part_two = lax.psum_scatter(g_kernel.reshape(-1), ("img", "ch"), tiled=True)
    part_head = lax.psum_scatter(g_head.reshape(-1), ("img", "ch"), tiled=True)
    g_two = part_two * mask_two.astype(jnp.float32)
    root = math.sqrt(images)
    one = sparse_update(w_one, g_one, mom_one, avg_one, mask_one, rank_one, 1.3 * root)
    bno = dense_update(
        first_norm_params,
        jnp.stack([first_norm_gain, first_shift_bias]),
        mom_bn_one,
        avg_bn_one,
        8.0 * root,
    )
    two = sparse_update(w_two, g_two, mom_two, avg_two, mask_two, rank_two, 0.25 * root)
    bnt = dense_update(
        second_norm_params,
        jnp.stack([second_norm_gain, second_shift_bias]),
        mom_bn_two,
        avg_bn_two,
        root,
    )
    top_head = dense_update(w_head, part_head, mom_head, avg_head, 40.0)
    return (
        loss,
        one[0],
        one[1],
        one[2],
        one[3],
        one[4],
        bno[0],
        bno[1],
        bno[2],
        two[0],
        two[1],
        two[2],
        two[3],
        two[4],
        bnt[0],
        bnt[1],
        bnt[2],
        top_head[0],
        top_head[1],
        top_head[2],
        top_head[0].astype(jnp.bfloat16),
    )


def solution(mesh):
    in_specs = (
        P("img", None, None),
        P(("img", "ch")),
        P(("img", "ch")),
        P("img", None),
        P(None, "ch"),
        P(None, "ch"),
        P(None, "ch"),
        P(None, "ch"),
        P(None, "ch"),
        P(None, "ch"),
        P(None, "ch"),
        P(None, "ch"),
        P(("img", "ch")),
        P(("img", "ch")),
        P(("img", "ch")),
        P(("img", "ch")),
        P(("img", "ch")),
        P(),
        P(),
        P(),
        P(("img", "ch")),
        P(("img", "ch")),
        P(("img", "ch")),
    )
    out_specs = (
        P(),
        P(None, "ch"),
        P(None, "ch"),
        P(None, "ch"),
        P(None, "ch"),
        P(None, "ch"),
        P(None, "ch"),
        P(None, "ch"),
        P(None, "ch"),
        P(("img", "ch")),
        P(("img", "ch")),
        P(("img", "ch")),
        P(("img", "ch")),
        P(("img", "ch")),
        P(),
        P(),
        P(),
        P(("img", "ch")),
        P(("img", "ch")),
        P(("img", "ch")),
        P(("img", "ch")),
    )
    return jax.shard_map(shards, mesh=mesh, in_specs=in_specs, out_specs=out_specs, check_vma=False)
```

profile of v0, /device:TPU:0, one launch (start us, length us, event | category | flops | bytes accessed | tf_op | source)
XLA Modules:
  0.0 576.8 jit_solution(3067732156576850317)
XLA Ops:
  7.2 1.7 multiply_convert_fusion.3
  9.7 13.4 %all-gather = f32[8,8,2]{1,2,0:T(2,128)S(1)} all-gather(f32[1,8,2]{1,2,0:T(2,128)S(1)} %maximum_bitcast_fusion), channel_id=1, replica_groups=mesh['img'=4,'ch'=8] {'ch'}, dimensions={0}, use_global_device_ids=true | all-gather | bytes 576 | tf_op jit(solution)/shard_map/all_gather | solution.py:104
  23.8 9.1 %fusion.29 = (f32[64]{0:T(128)S(1)}, f32[64]{0:T(128)S(1)}, f32[64,3136]{1,0:T(8,128)S(1)}) fusion(bf16[3136,2048]{1,0:T(8,128)(2,1)} %bitcast.114, f32[2048,64]{0,1:T(8,128)} %param.27, s32[2048,64]{0,1:T(8,128)} %param.30), kind=kOutput, calls=%fused_computation.118 | convolution fusion | flops 823078784 | bytes 14696960 | tf_op jit(solution)/shard_map/dot_general | solution.py:116
  32.9 10.7 %all-reduce.16 = (f32[]{:T(128)}, f32[64]{0:T(128)S(1)}, f32[64]{0:T(128)S(1)}) all-reduce(f32[]{:T(128)} %slice_reduce_fusion, f32[64]{0:T(128)S(1)} %get-tuple-element.26, f32[64]{0:T(128)S(1)} %get-tuple-element.25), channel_id=1, replica_groups=mesh['img'=4,'ch'=8] {'img'}, use_global_device_ids=true, to_apply=%region_2.3 | all-reduce | flops 129 | bytes 1032 | tf_op jit(solution)/shard_map/psum | solution.py:117
  45.1 2.4 copy.93
  48.8 3.5 all-to-all-start
  52.4 61.0 %all-gather.1 = bf16[32,1,16000]{2,1,0:T(2,128)(2,1)S(1)} all-gather(bf16[1,1,16000]{2,1,0:T(2,128)(2,1)S(1)} %reshape.227), channel_id=1, replica_groups=mesh['img'=4,'ch'=8] {'img','ch'}, dimensions={0}, use_global_device_ids=true | all-gather | bytes 1056000 | tf_op jit(solution)/shard_map/all_gather | solution.py:111
  113.4 7.2 %reduce.3 = bf16[32,16000]{1,0:T(8,128)(2,1)} reduce(bf16[32,1,16000]{2,1,0:T(2,128)(2,1)S(1)} %all-gather.1, bf16[]{:T(256)} %constant.97), dimensions={1}, to_apply=%all-gather.1.reduce_sub_computation | reduce | bytes 2048002 | tf_op jit(solution)/shard_map/all_gather | solution.py:111
  120.6 3.7 reshape.209
  124.5 1.7 reshape.232
  126.2 1.7 copy.95
  136.4 8.5 %reshape.207 = bf16[4608,512]{1,0:T(8,128)(2,1)} reshape(bf16[2359296]{0:T(1024)(128)(2,1)} %all-gather.4.cloned.1.call-done) | data formatting | bytes 9437184 | tf_op jit(solution)/shard_map/reshape | solution.py:112
  144.9 5.5 fusion.30
  150.4 39.6 %all-reduce.13 = (f32[512]{0:T(512)S(1)}, f32[512]{0:T(512)S(1)}) all-reduce(f32[512]{0:T(512)S(1)} %get-tuple-element.28, f32[512]{0:T(512)S(1)} %get-tuple-element.27), channel_id=1, replica_groups=mesh['img'=4,'ch'=8] {'img','ch'}, use_global_device_ids=true, to_apply=%region_10.11 | all-reduce | flops 1024 | bytes 8192 | tf_op jit(solution)/shard_map/psum | solution.py:145
  193.7 39.7 %all-reduce.12 = (f32[]{:T(128)}, f32[512]{0:T(512)S(1)}, f32[512]{0:T(512)S(1)}) all-reduce(f32[]{:T(128)} %get-tuple-element.57, f32[512]{0:T(512)S(1)} %get-tuple-element.22, f32[512]{0:T(512)S(1)} %get-tuple-element.21), channel_id=1, replica_groups=mesh['img'=4,'ch'=8] {'img','ch'}, use_global_device_ids=true, to_apply=%region_16.17 | all-reduce | flops 1025 | bytes 8200 | tf_op jit(solution)/shard_map/psum | solution.py:175
  233.4 4.7 fusion.27
  240.9 2.9 reshape.233
  243.9 3.5 all-to-all-start.1
  247.4 8.0 %convolution_bitcast_fusion = f32[576,4,8,128]{3,2,1,0:T(8,128)} fusion(bf16[392,4608]{1,0:T(8,128)(2,1)} %constant_dynamic-update-slice_fusion, f32[392,512]{1,0:T(8,128)S(1)} %get-tuple-element.89, f32[512]{0:T(512)S(1)} %get-tuple-element.32, f32[512]{0:T(512)S(1)} %broadcast_multiply_fusion, f32[512]{0:T(512)S(1)} %copy-done.39, ...), kind=kOutput, calls=%fused_computation | convolution fusion | flops 1853300736 | bytes 13883392 | tf_op jit(solution)/shard_map/pk,pc->kc/dot_general | solution.py:68
  255.4 9.8 %copy.105 = f32[576,4,8,128]{3,1,2,0:T(4,128)} copy(f32[576,4,8,128]{3,2,1,0:T(8,128)} %convolution_bitcast_fusion) | data formatting | bytes 18874368
  265.1 3.2 reshape.234
  271.3 1.9 copy.100
  273.8 10.4 %all-reduce.15 = (f32[64]{0:T(128)S(1)}, f32[64]{0:T(128)S(1)}) all-reduce(f32[64]{0:T(128)S(1)} %get-tuple-element.24, f32[64]{0:T(128)S(1)} %get-tuple-element.23), channel_id=1, replica_groups=mesh['img'=4,'ch'=8] {'img'}, use_global_device_ids=true, to_apply=%region_24.25 | all-reduce | flops 128 | bytes 1024 | tf_op jit(solution)/shard_map/psum | solution.py:207
  284.3 7.8 %fusion = bf16[2048,64]{0,1:T(8,128)(2,1)} fusion(bf16[3136,2048]{1,0:T(8,128)(2,1)} %bitcast.115, f32[3136,64]{0,1:T(8,128)S(1)} %get-tuple-element.56, f32[64,3136]{1,0:T(8,128)S(1)} %get-tuple-element.88, f32[64]{0:T(128)S(1)} %get-tuple-element.38, f32[64]{0:T(128)S(1)} %broadcast_multiply_fusion.2, f32[64]{0:T(128)S(1)} %copy-done.25, ...), kind=kOutput, calls=%fused_computation.2 | convolution fusion | flops 823820288 | bytes 14714112 | tf_op jit(solution)/shard_map/pk,pc->kc/dot_general | solution.py:68
  293.0 3.2 reshape.222
  300.4 34.6 %all-reduce.20.cloned.1.call-done = bf16[2048,64]{0,1:T(8,128)(2,1)} async-done(((bf16[2048,64]{0,1:T(8,128)(2,1)}), bf16[2048,64]{0,1:T(8,128)(2,1)}) %all-reduce.20.cloned.1.call-update) | async-done | bytes 262160 | tf_op jit(solution)/shard_map/psum | solution.py:223
  335.1 2.1 fusion.33
  337.2 2.1 add_multiply_fusion
  339.2 223.9 %all-reduce.22.cloned.1.call-done = (f32[2359296]{0:T(1024)}, f32[512000]{0:T(1024)}) async-done(((f32[2359296]{0:T(1024)}, f32[512000]{0:T(1024)}), (f32[2359296]{0:T(1024)}, f32[512000]{0:T(1024)})) %all-reduce.22.cloned.1.call-update) | async-done | bytes 11485200
  563.1 1.9 fusion.32
  565.1 1.8 add_multiply_fusion.1
  566.9 1.6 fusion.31
  (147 shorter events, 29.4 us)
Async XLA Ops:
  7.2 129.2 %all-gather.4.cloned.1.call-start = ((), (), s32[]{:S(2)}) async-start(), calls=%async_computation.2 | async-start | bytes 4866048 | tf_op jit(solution)/shard_map/all_gather | solution.py:110
  23.8 19.8 %copy-start.21 = (f32[2,64]{1,0:T(2,128)S(1)}, f32[2,64]{1,0:T(2,128)}, u32[]{:S(2)}) copy-start(f32[2,64]{1,0:T(2,128)} %param.32) | copy-start | bytes 1540
  32.9 19.4 %copy-start.10 = (f32[16000]{0:T(1024)S(1)}, f32[16000]{0:T(1024)}, u32[]{:S(2)}) copy-start(f32[16000]{0:T(1024)} %param.43) | copy-start | bytes 192004
  48.8 75.7 %all-to-all-start = ((bf16[8,2,12544]{2,1,0:T(2,128)(2,1)}), bf16[8,2,12544]{2,1,0:T(2,128)(2,1)S(1)}, u32[]{:S(2)}, u32[]{:S(2)}) async-start(bf16[8,2,12544]{2,1,0:T(2,128)(2,1)} %reshape.231), calls=%async_computation | async-start | bytes 802816 | tf_op jit(solution)/shard_map/all_to_all | solution.py:131
  52.4 71.9 %copy-start.42 = (s32[1,64]{1,0:T(1,128)S(1)}, s32[1,64]{1,0:T(1,128)}, u32[]{:S(2)}) copy-start(s32[1,64]{1,0:T(1,128)} %param.26) | copy-start | bytes 772
  52.4 72.1 %copy-start.11 = (f32[2,512]{1,0:T(2,128)S(1)}, f32[2,512]{1,0:T(2,128)}, u32[]{:S(2)}) copy-start(f32[2,512]{1,0:T(2,128)} %param.40) | copy-start | bytes 12292
  124.5 66.2 %copy-start.32 = (s32[8]{0:T(128)}, s32[8]{0:T(128)S(1)}, u32[]{:S(2)}) copy-start(s32[8]{0:T(128)S(1)} %convert_bitcast_fusion) | copy-start | bytes 100
  190.0 48.1 %copy-start.38 = (f32[512]{0:T(512)}, f32[512]{0:T(512)S(1)}, u32[]{:S(2)}) copy-start(f32[512]{0:T(512)S(1)} %get-tuple-element.78) | copy-start | bytes 6148
  233.4 4.7 copy-start.19
  233.4 14.0 %copy-start.36 = (f32[512]{0:T(512)}, f32[512]{0:T(512)S(1)}, u32[]{:S(2)}) copy-start(f32[512]{0:T(512)S(1)} %get-tuple-element.32) | copy-start | bytes 6148
  239.4 8.0 %copy-start.39 = (f32[512]{0:T(512)S(1)}, f32[512]{0:T(512)}, u32[]{:S(2)}) copy-start(f32[512]{0:T(512)} %copy-done.38) | copy-start | bytes 6148
  243.9 21.3 %all-to-all-start.1 = ((bf16[8,2,12544]{2,1,0:T(2,128)(2,1)}), bf16[8,2,12544]{2,1,0:T(2,128)(2,1)S(1)}, u32[]{:S(2)}, u32[]{:S(2)}) async-start(bf16[8,2,12544]{2,1,0:T(2,128)(2,1)} %reshape.233), calls=%async_computation.1 | async-start | bytes 802816 | tf_op jit(solution)/shard_map/all_to_all | solution.py:203
  247.3 87.8 %all-reduce.20.cloned.1.call-start = ((), (), s32[]{:S(2)}) async-start(), calls=%async_computation.3 | async-start | bytes 524288 | tf_op jit(solution)/shard_map/psum | solution.py:223
  269.4 3.8 copy-start.14
  269.4 3.8 copy-start.16
  269.4 3.8 copy-start.27
  269.5 3.8 copy-start.29
  269.8 14.4 %copy-start.25 = (f32[64]{0:T(128)S(1)}, f32[64]{0:T(128)}, u32[]{:S(2)}) copy-start(f32[64]{0:T(128)} %get-tuple-element.83) | copy-start | bytes 772
  284.2 8.2 %copy-start.18 = (f32[8]{0:T(128)S(1)}, f32[8]{0:T(128)}, u32[]{:S(2)}) copy-start(f32[8]{0:T(128)} %copy-done.17) | copy-start | bytes 100
  284.2 8.2 %copy-start.24 = (f32[8]{0:T(128)S(1)}, f32[8]{0:T(128)}, u32[]{:S(2)}) copy-start(f32[8]{0:T(128)} %copy-done.23) | copy-start | bytes 100
  284.2 8.2 %copy-start.33 = (s32[8]{0:T(128)S(1)}, s32[8]{0:T(128)}, u32[]{:S(2)}) copy-start(s32[8]{0:T(128)} %copy-done.32) | copy-start | bytes 100
  284.2 8.2 %copy-start.35 = (f32[8]{0:T(128)S(1)}, f32[8]{0:T(128)}, u32[]{:S(2)}) copy-start(f32[8]{0:T(128)} %copy-done.34) | copy-start | bytes 100
  292.1 271.0 %all-reduce.22.cloned.1.call-start = ((), (), s32[]{:S(2)}) async-start(), calls=%async_computation.4 | async-start | bytes 22970368
  296.2 3.0 copy-start.12
  296.2 3.6 copy-start.22
  296.3 3.6 copy-start.40
  296.3 3.6 copy-start.41
  296.3 38.8 %copy-start.4 = (f32[2048,64]{0,1:T(8,128)S(1)}, f32[2048,64]{0,1:T(8,128)}, u32[]{:S(2)}) copy-start(f32[2048,64]{0,1:T(8,128)} %param.27) | copy-start | bytes 1572868
  296.3 38.8 %copy-start.8 = (f32[2048,64]{0,1:T(8,128)S(1)}, f32[2048,64]{0,1:T(8,128)}, u32[]{:S(2)}) copy-start(f32[2048,64]{0,1:T(8,128)} %param.28) | copy-start | bytes 1572868
  297.4 265.7 %copy-start.7 = (f32[73728]{0:T(1024)S(1)}, f32[73728]{0:T(1024)}, u32[]{:S(2)}) copy-start(f32[73728]{0:T(1024)} %param.35) | copy-start | bytes 884740
  337.1 232.9 %copy-start.3 = (f32[2048,64]{0,1:T(8,128)}, f32[2048,64]{0,1:T(8,128)S(1)}, u32[]{:S(2)}) copy-start(f32[2048,64]{0,1:T(8,128)S(1)} %get-tuple-element.55) | copy-start | bytes 1572868
  565.1 5.0 copy-start.6
  (16 other events, 29.9 us)
Sparse Core Ops, SparseCore 0:
  11.6 73.5 all-gather.3
  292.2 42.8 all-reduce.19
  342.6 220.4 all-reduce.21
where the time goes:
time: 582 us; the launch traced here: 577 us
  waiting for transfers between devices  259 us (45%)
  blocking collectives  175 us (30%)
  local copies, waits for them, and re-layouts  55.6 us (10%)
  matrix products  37 us (6%)
  other arithmetic  29.1 us (5%)
  between operations  14.7 us (3%)
  starting transfers between devices  7.28 us (1%)
    unnamed x4, waiting for transfers between devices  224 us
    all_gather x1, blocking collectives, shards(): lax.all_gather(w_head.astype(jnp.bfloat16), ('img', 'ch'), axis=0, tiled=...  61 us
    psum x1, blocking collectives, shards(): lax.psum((jnp.sum(second_output_gradient, axis=0), jnp.sum(second_output_...  39.7 us
    psum x1, blocking collectives, shards(): lax.psum((jnp.sum(second_conv_output, axis=0), jnp.sum(second_conv_output...  39.6 us
    psum x1, waiting for transfers between devices, shards(): lax.psum(contract_rows(rows, first_preact_gradient).astype(jnp.bfloat16),...  34.6 us
    unnamed x101, local copies, waits for them, and re-layouts  26.9 us
    dot_general x3, matrix products, contract_rows(): jnp.einsum('pk,pc->kc', left, right, preferred_element_type=jnp.float32)  16.3 us
    all_gather x1, blocking collectives, shards(): slot_info = lax.all_gather(slot_info, 'ch', axis=1, tiled=True)  13.4 us
  transfers between devices with their start and end apart: 5, of which 2 were waited for; matrix products, arithmetic and copies ran while one was open for 12% of the time, Pallas kernels for 0%

commit v1 on v0

--- a/solution.py
+++ b/solution.py
@@ -220,8 +220,9 @@
         first_norm_gain,
         first_element_count,
     ).astype(jnp.bfloat16)
-    g_filt = lax.psum(
-        contract_rows(rows, first_preact_gradient).astype(jnp.bfloat16), "img"
+    g_filt = jnp.sum(
+        lax.all_gather(contract_rows(rows, first_preact_gradient).astype(jnp.bfloat16), "img"),
+        axis=0,
     ).astype(jnp.float32)
     g_one = g_filt * mask_one.astype(jnp.float32)
     part_two = lax.psum_scatter(g_kernel.reshape(-1), ("img", "ch"), tiled=True)

time: 582 us -> 557 us (0.957)
  waiting for transfers between devices: 259 us -> 218 us
  blocking collectives: 175 us -> 191 us
    psum x1 -> x0, waiting for transfers between devices: 34.6 us -> none  [shards(): lax.psum(contract_rows(rows, first_preact_gradient).astype(jnp.bfloat16),...]
    all_to_all x0 -> x1, blocking collectives: none -> 15.6 us  [shards(): lax.all_to_all(d_act_in, 'ch', split_axis=2, concat_axis=1, tiled=True)]
    unnamed x4, waiting for transfers between devices: 224 us -> 218 us
    unnamed x101 -> x123, local copies, waits for them, and re-layouts: 26.9 us -> 27.2 us
  transfers between devices with their start and end apart: 5 -> 4, of which waited for: 2 -> 1; matrix products, arithmetic and copies ran while one was open for 12% -> 13% of each run, Pallas kernels for 0% -> 0%
where the time goes in v1:
time: 557 us; the launch traced here: 552 us
  waiting for transfers between devices  218 us (39%)
  blocking collectives  191 us (34%)
  local copies, waits for them, and re-layouts  59.6 us (11%)
  matrix products  36.8 us (7%)
  other arithmetic  28.3 us (5%)
  between operations  14.6 us (3%)
    unnamed x4, waiting for transfers between devices  218 us
    all_gather x1, blocking collectives, shards(): lax.all_gather(w_head.astype(jnp.bfloat16), ('img', 'ch'), axis=0, tiled=...  60.9 us
    psum x1, blocking collectives, shards(): lax.psum((jnp.sum(second_conv_output, axis=0), jnp.sum(second_conv_output...  39.7 us
    psum x1, blocking collectives, shards(): lax.psum((jnp.sum(second_output_gradient, axis=0), jnp.sum(second_output_...  39.4 us
    unnamed x123, local copies, waits for them, and re-layouts  27.2 us
    dot_general x3, matrix products, contract_rows(): jnp.einsum('pk,pc->kc', left, right, preferred_element_type=jnp.float32)  16.1 us
    all_to_all x1, blocking collectives, shards(): lax.all_to_all(d_act_in, 'ch', split_axis=2, concat_axis=1, tiled=True)  15.6 us
    all_gather x1, blocking collectives, shards(): slot_info = lax.all_gather(slot_info, 'ch', axis=1, tiled=True)  13.4 us
  transfers between devices with their start and end apart: 4, of which 1 were waited for; matrix products, arithmetic and copies ran while one was open for 13% of the time, Pallas kernels for 0%

profile of v1, /device:TPU:0, one launch (start us, length us, event | category | flops | bytes accessed | tf_op | source)
XLA Modules:
  0.0 551.6 jit_solution(15930042460276161133)
XLA Ops:
  7.2 1.7 multiply_convert_fusion.3
  9.7 13.4 %all-gather.1 = f32[8,8,2]{1,2,0:T(2,128)S(1)} all-gather(f32[1,8,2]{1,2,0:T(2,128)S(1)} %maximum_bitcast_fusion), channel_id=1, replica_groups=mesh['img'=4,'ch'=8] {'ch'}, dimensions={0}, use_global_device_ids=true | all-gather | bytes 576 | tf_op jit(solution)/shard_map/all_gather | solution.py:104
  23.8 9.1 %fusion.29 = (f32[64]{0:T(128)S(1)}, f32[64]{0:T(128)S(1)}, f32[64,3136]{1,0:T(8,128)S(1)}) fusion(bf16[3136,2048]{1,0:T(8,128)(2,1)} %bitcast.116, f32[2048,64]{0,1:T(8,128)} %param.27, s32[2048,64]{0,1:T(8,128)} %param.30), kind=kOutput, calls=%fused_computation.118 | convolution fusion | flops 823078784 | bytes 14696960 | tf_op jit(solution)/shard_map/dot_general | solution.py:116
  32.9 10.7 %all-reduce.16 = (f32[]{:T(128)}, f32[64]{0:T(128)S(1)}, f32[64]{0:T(128)S(1)}) all-reduce(f32[]{:T(128)} %slice_reduce_fusion, f32[64]{0:T(128)S(1)} %get-tuple-element.26, f32[64]{0:T(128)S(1)} %get-tuple-element.25), channel_id=1, replica_groups=mesh['img'=4,'ch'=8] {'img'}, use_global_device_ids=true, to_apply=%region_2.3 | all-reduce | flops 129 | bytes 1032 | tf_op jit(solution)/shard_map/psum | solution.py:117
  45.1 2.4 copy.93
  48.8 3.5 all-to-all-start
  52.4 60.9 %all-gather.2 = bf16[32,1,16000]{2,1,0:T(2,128)(2,1)S(1)} all-gather(bf16[1,1,16000]{2,1,0:T(2,128)(2,1)S(1)} %reshape.228), channel_id=1, replica_groups=mesh['img'=4,'ch'=8] {'img','ch'}, dimensions={0}, use_global_device_ids=true | all-gather | bytes 1056000 | tf_op jit(solution)/shard_map/all_gather | solution.py:111
  113.3 7.2 %reduce.4 = bf16[32,16000]{1,0:T(8,128)(2,1)} reduce(bf16[32,1,16000]{2,1,0:T(2,128)(2,1)S(1)} %all-gather.2, bf16[]{:T(256)} %constant.98), dimensions={1}, to_apply=%all-gather.2.reduce_sub_computation | reduce | bytes 2048002 | tf_op jit(solution)/shard_map/all_gather | solution.py:111
  120.5 3.6 reshape.209
  124.4 1.7 reshape.233
  126.1 1.7 copy.95
  136.3 8.5 %reshape.207 = bf16[4608,512]{1,0:T(8,128)(2,1)} reshape(bf16[2359296]{0:T(1024)(128)(2,1)} %all-gather.6.cloned.1.call-done) | data formatting | bytes 9437184 | tf_op jit(solution)/shard_map/reshape | solution.py:112
  144.8 5.5 fusion.30
  150.3 39.7 %all-reduce.13 = (f32[512]{0:T(512)S(1)}, f32[512]{0:T(512)S(1)}) all-reduce(f32[512]{0:T(512)S(1)} %get-tuple-element.28, f32[512]{0:T(512)S(1)} %get-tuple-element.27), channel_id=1, replica_groups=mesh['img'=4,'ch'=8] {'img','ch'}, use_global_device_ids=true, to_apply=%region_10.11 | all-reduce | flops 1024 | bytes 8192 | tf_op jit(solution)/shard_map/psum | solution.py:145
  194.2 39.4 %all-reduce.12 = (f32[]{:T(128)}, f32[512]{0:T(512)S(1)}, f32[512]{0:T(512)S(1)}) all-reduce(f32[]{:T(128)} %get-tuple-element.57, f32[512]{0:T(512)S(1)} %get-tuple-element.22, f32[512]{0:T(512)S(1)} %get-tuple-element.21), channel_id=1, replica_groups=mesh['img'=4,'ch'=8] {'img','ch'}, use_global_device_ids=true, to_apply=%region_16.17 | all-reduce | flops 1025 | bytes 8200 | tf_op jit(solution)/shard_map/psum | solution.py:175
  233.6 4.7 fusion.27
  241.1 2.1 reshape.234
  243.3 15.6 %all_to_all.24 = bf16[8,2,12544]{2,1,0:T(2,128)(2,1)S(1)} all-to-all(bf16[8,2,12544]{2,1,0:T(2,128)(2,1)S(1)} %reshape.234), channel_id=1, replica_groups=mesh['img'=4,'ch'=8] {'ch'}, dimensions={0} | all-to-all | bytes 802816 | tf_op jit(solution)/shard_map/all_to_all | solution.py:203
  258.9 3.2 reshape.235
  262.1 1.9 copy.98
  267.0 1.9 copy.100
  269.5 11.2 %all-reduce.15 = (f32[64]{0:T(128)S(1)}, f32[64]{0:T(128)S(1)}) all-reduce(f32[64]{0:T(128)S(1)} %get-tuple-element.24, f32[64]{0:T(128)S(1)} %get-tuple-element.23), channel_id=1, replica_groups=mesh['img'=4,'ch'=8] {'img'}, use_global_device_ids=true, to_apply=%region_24.25 | all-reduce | flops 128 | bytes 1024 | tf_op jit(solution)/shard_map/psum | solution.py:207
  281.3 7.8 %fusion = bf16[2048,64]{0,1:T(8,128)(2,1)} fusion(bf16[3136,2048]{1,0:T(8,128)(2,1)} %bitcast.117, f32[3136,64]{0,1:T(8,128)S(1)} %get-tuple-element.56, f32[64,3136]{1,0:T(8,128)S(1)} %get-tuple-element.88, f32[64]{0:T(128)S(1)} %get-tuple-element.38, f32[64]{0:T(128)S(1)} %broadcast_multiply_fusion.2, f32[64]{0:T(128)S(1)} %copy-done.31, ...), kind=kOutput, calls=%fused_computation.2 | convolution fusion | flops 823820288 | bytes 14714112 | tf_op jit(solution)/shard_map/pk,pc->kc/dot_general | solution.py:68
  289.2 7.8 %convolution_bitcast_fusion = f32[576,4,8,128]{3,2,1,0:T(8,128)} fusion(bf16[392,4608]{1,0:T(8,128)(2,1)} %constant_dynamic-update-slice_fusion, f32[392,512]{1,0:T(8,128)S(1)} %get-tuple-element.89, f32[512]{0:T(512)S(1)} %copy-done.43, f32[512]{0:T(512)S(1)} %copy-done.46, f32[512]{0:T(512)S(1)} %copy-done.48, f32[512]{0:T(512)S(1)} %get-tuple-element.79, ...), kind=kOutput, calls=%fused_computation | convolution fusion | flops 1853300736 | bytes 13883392 | tf_op jit(solution)/shard_map/pk,pc->kc/dot_general | solution.py:68
  297.0 9.8 %copy.105 = f32[576,4,8,128]{3,1,2,0:T(4,128)} copy(f32[576,4,8,128]{3,2,1,0:T(8,128)} %convolution_bitcast_fusion) | data formatting | bytes 18874368
  307.4 3.3 reshape.222
  314.9 1.8 reshape.225
  316.8 2.2 reduce_sum.152
  319.0 2.3 fusion.33
  322.1 217.7 %all-reduce.19.cloned.1.call-done = (f32[2359296]{0:T(1024)}, f32[512000]{0:T(1024)}) async-done(((f32[2359296]{0:T(1024)}, f32[512000]{0:T(1024)}), (f32[2359296]{0:T(1024)}, f32[512000]{0:T(1024)})) %all-reduce.19.cloned.1.call-update) | async-done | bytes 11485200
  539.9 1.9 fusion.32
  542.6 1.6 fusion.31
  (170 shorter events, 31.1 us)
Async XLA Ops:
  7.2 129.1 %all-gather.6.cloned.1.call-start = ((), (), s32[]{:S(2)}) async-start(), calls=%async_computation.2 | async-start | bytes 4866048 | tf_op jit(solution)/shard_map/all_gather | solution.py:110
  23.8 19.7 %copy-start.25 = (f32[2,64]{1,0:T(2,128)S(1)}, f32[2,64]{1,0:T(2,128)}, u32[]{:S(2)}) copy-start(f32[2,64]{1,0:T(2,128)} %param.32) | copy-start | bytes 1540
  32.9 19.4 %copy-start.11 = (f32[16000]{0:T(1024)S(1)}, f32[16000]{0:T(1024)}, u32[]{:S(2)}) copy-start(f32[16000]{0:T(1024)} %param.43) | copy-start | bytes 192004
  48.8 75.6 %all-to-all-start = ((bf16[8,2,12544]{2,1,0:T(2,128)(2,1)}), bf16[8,2,12544]{2,1,0:T(2,128)(2,1)S(1)}, u32[]{:S(2)}, u32[]{:S(2)}) async-start(bf16[8,2,12544]{2,1,0:T(2,128)(2,1)} %reshape.232), calls=%async_computation | async-start | bytes 802816 | tf_op jit(solution)/shard_map/all_to_all | solution.py:131
  52.2 262.7 %all-gather.8.cloned.1.call-start = ((), (), s32[]{:S(2)}) async-start(), calls=%async_computation.3 | async-start | bytes 1310720 | tf_op jit(solution)/shard_map/all_gather | solution.py:224
  52.4 71.8 %copy-start.53 = (s32[1,64]{1,0:T(1,128)S(1)}, s32[1,64]{1,0:T(1,128)}, u32[]{:S(2)}) copy-start(s32[1,64]{1,0:T(1,128)} %param.26) | copy-start | bytes 772
  52.4 72.0 %copy-start.15 = (f32[2,512]{1,0:T(2,128)S(1)}, f32[2,512]{1,0:T(2,128)}, u32[]{:S(2)}) copy-start(f32[2,512]{1,0:T(2,128)} %param.40) | copy-start | bytes 12292
  124.3 66.3 %copy-start.38 = (s32[8]{0:T(128)}, s32[8]{0:T(128)S(1)}, u32[]{:S(2)}) copy-start(s32[8]{0:T(128)S(1)} %convert_bitcast_fusion) | copy-start | bytes 100
  190.0 48.3 %copy-start.47 = (f32[512]{0:T(512)}, f32[512]{0:T(512)S(1)}, u32[]{:S(2)}) copy-start(f32[512]{0:T(512)S(1)} %get-tuple-element.78) | copy-start | bytes 6148
  190.6 47.7 %copy-start.21 = (f32[8]{0:T(128)}, f32[8]{0:T(128)S(1)}, u32[]{:S(2)}) copy-start(f32[8]{0:T(128)S(1)} %get-tuple-element.90) | copy-start | bytes 100
  233.6 4.8 copy-start.45
  263.9 5.0 copy-start.18
  263.9 5.0 copy-start.20
  263.9 5.0 copy-start.33
  263.9 5.0 copy-start.35
  265.4 15.8 %copy-start.31 = (f32[64]{0:T(128)S(1)}, f32[64]{0:T(128)}, u32[]{:S(2)}) copy-start(f32[64]{0:T(128)} %get-tuple-element.83) | copy-start | bytes 772
  280.7 8.4 %copy-start.27 = (f32[64]{0:T(128)}, f32[64]{0:T(128)S(1)}, u32[]{:S(2)}) copy-start(f32[64]{0:T(128)S(1)} %get-tuple-element.38) | copy-start | bytes 772
  281.3 7.9 %copy-start.43 = (f32[512]{0:T(512)S(1)}, f32[512]{0:T(512)}, u32[]{:S(2)}) copy-start(f32[512]{0:T(512)} %copy-done.42) | copy-start | bytes 6148
  281.3 7.9 %copy-start.46 = (f32[512]{0:T(512)S(1)}, f32[512]{0:T(512)}, u32[]{:S(2)}) copy-start(f32[512]{0:T(512)} %copy-done.45) | copy-start | bytes 6148
  281.3 8.0 %copy-start.48 = (f32[512]{0:T(512)S(1)}, f32[512]{0:T(512)}, u32[]{:S(2)}) copy-start(f32[512]{0:T(512)} %copy-done.47) | copy-start | bytes 6148
  289.1 250.7 %all-reduce.19.cloned.1.call-start = ((), (), s32[]{:S(2)}) async-start(), calls=%async_computation.4 | async-start | bytes 22970368
  297.0 9.9 %copy-start.22 = (f32[8]{0:T(128)S(1)}, f32[8]{0:T(128)}, u32[]{:S(2)}) copy-start(f32[8]{0:T(128)} %copy-done.21) | copy-start | bytes 100
  297.0 9.9 %copy-start.30 = (f32[8]{0:T(128)S(1)}, f32[8]{0:T(128)}, u32[]{:S(2)}) copy-start(f32[8]{0:T(128)} %copy-done.29) | copy-start | bytes 100
  297.0 9.9 %copy-start.39 = (s32[8]{0:T(128)S(1)}, s32[8]{0:T(128)}, u32[]{:S(2)}) copy-start(s32[8]{0:T(128)} %copy-done.38) | copy-start | bytes 100
  297.0 9.9 %copy-start.41 = (f32[8]{0:T(128)S(1)}, f32[8]{0:T(128)}, u32[]{:S(2)}) copy-start(f32[8]{0:T(128)} %copy-done.40) | copy-start | bytes 100
  310.8 8.2 %copy-start.4 = (f32[2048,64]{0,1:T(8,128)S(1)}, f32[2048,64]{0,1:T(8,128)}, u32[]{:S(2)}) copy-start(f32[2048,64]{0,1:T(8,128)} %param.27) | copy-start | bytes 1572868
  316.8 223.1 %copy-start.7 = (f32[73728]{0:T(1024)S(1)}, f32[73728]{0:T(1024)}, u32[]{:S(2)}) copy-start(f32[73728]{0:T(1024)} %param.35) | copy-start | bytes 884740
  321.2 223.6 %copy-start.3 = (f32[2048,64]{0,1:T(8,128)}, f32[2048,64]{0,1:T(8,128)S(1)}, u32[]{:S(2)}) copy-start(f32[2048,64]{0,1:T(8,128)S(1)} %get-tuple-element.55) | copy-start | bytes 1572868
  321.2 220.6 %copy-start.9 = (f32[73728]{0:T(1024)S(1)}, f32[73728]{0:T(1024)}, u32[]{:S(2)}) copy-start(f32[73728]{0:T(1024)} %param.37) | copy-start | bytes 884740
  321.2 221.4 %copy-start.12 = (f32[16000]{0:T(1024)S(1)}, f32[16000]{0:T(1024)}, u32[]{:S(2)}) copy-start(f32[16000]{0:T(1024)} %param.43) | copy-start | bytes 192004
  321.2 221.4 %copy-start.14 = (f32[16000]{0:T(1024)S(1)}, f32[16000]{0:T(1024)}, u32[]{:S(2)}) copy-start(f32[16000]{0:T(1024)} %param.44) | copy-start | bytes 192004
  321.3 223.0 %copy-start.13 = (f32[16000]{0:T(1024)S(1)}, f32[16000]{0:T(1024)}, u32[]{:S(2)}) copy-start(f32[16000]{0:T(1024)} %param.45) | copy-start | bytes 192004
  (26 other events, 60.3 us)
Sparse Core Ops, SparseCore 0:
  11.6 73.5 all-gather.5
  289.3 23.6 all-gather.7
  319.4 220.4 all-reduce.18
